TPU v7x, 256 devices: a whole 4x4x8 slice. The times are simulated.
256 devices in a mesh: dp: 16 (over x, z_hi, core), tensor: 16 (over y, z_lo).
Axes of the slice: x: 4, y: 4, z: 8 (z_hi: 2, z_lo: 4; z = z_hi * 4 + z_lo), core: 2. Of those that a mesh axis runs over, the one named last changes fastest.
Arguments:
- attn_out: bfloat16 [2048, 16384], P('dp', 'tensor'), may hold values from -6 to 6
- teacher_resid: bfloat16 [2048, 16384], P('tensor', 'dp'), may hold values from -6 to 6
- w_out: bfloat16 [16384, 16384], P('tensor', 'dp'), may hold values from -0.046875 to 0.046875
- projection: bfloat16 [16384, 4096], P('dp', 'tensor'), may hold values from -0.046875 to 0.046875
- student_in: bfloat16 [2048, 4096], P('dp', 'tensor'), may hold values from -6 to 6
- gate_act: bfloat16 [2048, 14336], P('dp', 'tensor'), may hold values from -6 to 6
- up_act: bfloat16 [2048, 14336], P('dp', 'tensor'), may hold values from -6 to 6
- w_down: bfloat16 [14336, 4096], P('tensor'), may hold values from -0.046875 to 0.046875
Outputs:
- gate_grad: float32 [2048, 14336], P('dp', 'tensor')
- up_grad: float32 [2048, 14336], P('dp', 'tensor')
- down_grad: float32 [14336, 4096], P('tensor', 'dp')
All inputs are finite; a program needn't handle non-finite values.
Results may differ from a plain program's by a relative error of at most 0.029.
Values may be sent and summed in bfloat16 or wider, within the bound.
A program may use at most 128 MiB of HBM per device.

v0:
```python
import functools

import jax
import jax.numpy as jnp
from jax import lax
from jax.experimental import pallas as pl
from jax.experimental.pallas import tpu as pltpu
from jax.sharding import PartitionSpec as P

MESH = pl.DeviceIdType.MESH
F32 = jnp.float32
BF16 = jnp.bfloat16

Q = 4
TOK = 128
S = TOK // Q
DK = 1024
DC = 256
DS = 4096
FF = 896
ORDER = ("own.0", "own.1", "student", "far.0", "own.2", "turn", "sib.0", "far.1", "own.3", "hown", "stf", "far.2", "mix.0", "sib.1", "stz", "far.3", "mix.1", "fwd.0", "fwd.1", "hfar", "z.0", "sib.2", "ste", "z.1", "mix.2", "sib.3", "state.0", "mix.3", "fwd.2", "state.1", "hsib", "fwd.3", "hend", "ally.0", "z.2", "ally.1", "z.3", "state.2", "allf.0", "map.0", "allf.1", "map.1", "state.3", "tgt.0", "tx.0", "ally.2", "tgt.1", "tx.1", "tz.0", "ally.3", "allf.2", "tz.1", "map.2", "mis.0", "mis.1", "mir.0", "ey.0", "allf.3", "map.3", "mir.1", "ey.1", "fy.0", "tgt.2", "fy.1", "ef.0", "tx.2", "tgt.3", "ef.1", "tz.2", "tx.3", "ff.0", "mis.2", "ff.1", "ee.0", "ee.1", "tz.3", "fe.0", "fe.1", "ey.2", "mir.2", "mis.3", "fy.2", "ef.2", "mir.3", "ey.3", "ff.2", "fy.3", "ee.2", "ef.3", "fe.2", "ff.3", "ee.3", "grads", "fe.3", "down")

A_SLOTS, B_SLOTS, C_SLOTS, D_SLOTS, E_SLOTS = 12, 9, 13, 5, 15
E_GATHER = 7
A0 = 0
B0 = A0 + A_SLOTS * Q
C0 = B0 + B_SLOTS * Q
D0 = C0 + C_SLOTS * Q
E0 = D0 + D_SLOTS * Q
SB0 = E0 + E_SLOTS * Q
H0 = SB0 + B_SLOTS
N_SLOTS = H0 + A_SLOTS


def kernel(
    attn, resid, w_out, proj, stud, gate, up, w_down,
    gate_grad, up_grad, down_grad,
    g, p1, y1, y2, r, zr, ta, p2, ds1, p3, dx, p4, p4b, dz,
    ma, mt, mb, hid, ht, sp, sy1, sy2, sr, szr, so,
    vw_out, vproj, vw_down, vturned, vresid, vstud, vgate, vup,
    ss, rs, ls,
):
    d = lax.axis_index("dp")
    t = lax.axis_index("tensor")
    x, zh, c = d // 4, lax.rem(d // 2, 2), lax.rem(d, 2)
    y, zl = t // 4, lax.rem(t, 4)

    def dev(x_, zh_, c_, y_, zl_):
        return ((x_ * 2 + zh_) * 2 + c_, y_ * 4 + zl_)

    def ring(a, k):
        return lax.rem(a + k, 4)

    sib = dev(x, zh, 1 - c, y, zl)
    far = dev(x, 1 - zh, c, y, zl)
    xs = [dev(ring(x, k), zh, c, y, zl) for k in (1, 2, 3)]
    zs = [dev(x, zh, c, y, ring(zl, k)) for k in (1, 2, 3)]
    yn, yp = dev(x, zh, c, ring(y, 1), zl), dev(x, zh, c, ring(y, 3), zl)
    mirror = (t, d)

    def load(i, src, dst):
        return pltpu.make_async_copy(src, dst, ls.at[i])

    own_a = [load(q, attn.at[pl.ds(q * S, S)], g.at[q, x, zh, c]) for q in range(Q)]
    l_gate = load(Q, gate, vgate)
    l_up = load(Q + 1, up, vup)
    l_down = load(Q + 2, w_down, vw_down)
    l_out = load(Q + 3, w_out, vw_out)
    l_proj = load(Q + 4, proj, vproj)
    l_resid = load(Q + 5, resid, vresid)
    l_stud = load(Q + 6, stud, vstud)
    for cp in [l_gate, l_up, l_down, l_out] + own_a + [l_proj, l_resid, l_stud]:
        cp.start()

    barrier = pltpu.get_barrier_semaphore()
    for peer in [sib, far, yn, yp] + xs + zs:
        pl.semaphore_signal(barrier, 1, device_id=peer, device_id_type=MESH)

    @pl.when(d != t)
    def _():
        pl.semaphore_signal(barrier, 1, device_id=mirror, device_id_type=MESH)

    pl.semaphore_wait(barrier, jnp.where(d != t, 11, 10))

    started = []

    def send(slot, src, dst, peer):
        cp = pltpu.make_async_remote_copy(
            src, dst, ss.at[slot], rs.at[slot], device_id=peer, device_id_type=MESH
        )
        cp.start()
        started.append(cp)
        return cp

    def gather_dp_own(base, own, place, place2):
        dst = place(x, zh, c)
        m = {}
        m["z"] = send(base, own, dst, far)
        for k in (1, 2, 3):
            m["x", k] = send(base + k, own, dst, xs[k - 1])
        m["s0"] = send(base + 4, own, dst, sib)
        return m

    def gather_dp_far(base, m, place, place2):
        m["z"].wait_recv()
        piece = place(x, 1 - zh, c)
        for k in (1, 2, 3):
            m["zx", k] = send(base + 4 + k, piece, piece, xs[k - 1])
        m["s1"] = send(base + 8, piece, piece, sib)

    def gather_dp_sib(base, m, place, place2):
        for k in (1, 3, 2):
            m["x", k].wait_recv()
            m["zx", k].wait_recv()
            piece = place2(ring(x, 4 - k), c)
            m["s", k] = send(base + 8 + k, piece, piece, sib)

    def gather_dp_end(m):
        m["s0"].wait_recv()
        m["s1"].wait_recv()
        for k in (1, 3, 2):
            m["s", k].wait_recv()

    def scatter_y_first(base, part, a1):
        far_y = ring(y, 2)
        m = {}
        m["h0"] = send(base, part.at[far_y, pl.ds(0, 2)], a1.at[0], yn)
        m["h1"] = send(base + 1, part.at[far_y, pl.ds(2, 2)], a1.at[1], yp)
        return m

    def scatter_y_raw(base, m, part, a2):
        m["r0"] = send(base + 2, part.at[ring(y, 1), pl.ds(2, 2)], a2.at[0, pl.ds(2, 2)], yn)
        m["r1"] = send(base + 3, part.at[ring(y, 3), pl.ds(0, 2)], a2.at[1, pl.ds(0, 2)], yp)

    def scatter_y_forward(base, m, part, a1, a2):
        for side, (lo, to, peer) in enumerate(((0, ring(y, 1), yn), (2, ring(y, 3), yp))):
            m["h%d" % side].wait_recv()
            for i in range(2):
                both = part[to, lo + i].astype(F32) + a1[side, i].astype(F32)
                part[to, lo + i] = both.astype(BF16)
            m["c%d" % side] = send(
                base + 4 + side, part.at[to, pl.ds(lo, 2)], a2.at[side, pl.ds(lo, 2)], peer
            )

    def scatter_z(base, m, part, a2, res, az):
        for n in ("r0", "r1", "c0", "c1"):
            m[n].wait_recv()
        for i in range(4):
            total = part[y, i].astype(F32) + a2[0, i].astype(F32) + a2[1, i].astype(F32)
            res[i] = total.astype(BF16)
        for k in (1, 2, 3):
            m["z", k] = send(base + 5 + k, res.at[ring(zl, k)], az.at[k - 1], zs[k - 1])

    def scatter_end(m, res, az):
        for k in (1, 2, 3):
            m["z", k].wait_recv()
        total = res[zl].astype(F32)
        for k in range(3):
            total += az[k].astype(F32)
        return total

    def gather_z(base, view, early=False):
        own = view(y, zl, 1)
        m = {("z", k): send(base + k - 1, own, own, zs[k - 1]) for k in (1, 2, 3)}
        m["early"] = early
        if early:
            m["y0", 0] = send(base + 3, own, own, yn)
            m["y1", 0] = send(base + 4, own, own, yp)
        return m

    def gather_y(base, m, view):
        if m["early"]:
            for k in (1, 3, 2):
                m["z", k].wait_recv()
                piece = view(y, ring(zl, 4 - k), 1)
                m["y0", k] = send(base + 3 + 2 * k, piece, piece, yn)
                m["y1", k] = send(base + 4 + 2 * k, piece, piece, yp)
        else:
            for k in (1, 2, 3):
                m["z", k].wait_recv()
            mine = view(y, 0, 4)
            m["y0", 0] = send(base + 3, mine, mine, yn)
            m["y1", 0] = send(base + 4, mine, mine, yp)

    def gather_forward(base, m, view):
        base += 11 if m["early"] else 5
        for side, (far_y, lo, peer) in enumerate(((ring(y, 3), 0, yn), (ring(y, 1), 2, yp))):
            for k in (0, 1, 3, 2) if m["early"] else (0,):
                m["y%d" % side, k].wait_recv()
            half = view(far_y, lo, 2)
            m["f%d" % side] = send(base + side, half, half, peer)

    def gather_end(m):
        m["f0"].wait_recv()
        m["f1"].wait_recv()

    A = [None] * Q
    B = [None] * Q
    C = [None] * Q
    D = [{} for _ in range(Q)]
    E = [None] * Q
    EM = [None] * Q

    def g_place(q):
        return lambda x_, zh_, c_: g.at[q, x_, zh_, c_]

    def g_place2(q):
        return lambda x_, c_: g.at[q, x_, :, c_]

    def ta_view(q):
        return lambda y_, lo, n: ta.at[q, y_, pl.ds(lo, n)]

    def ma_view(q):
        def view(y_, lo, n):
            start = pl.multiple_of((y_ * 4 + lo) * DC, DC)
            return ma.at[pl.ds(q * S, S), pl.ds(start, n * DC)]

        return view

    def mb_view(q):
        rows = pl.ds(q * S, S)

        def view(y_, lo, n):
            if n == 1:
                return mb.at[lax.rem(lo, 2), y_ * 2 + lo // 2, rows]
            if n == 2:
                return mb.at[:, y_ * 2 + lo // 2, rows]
            return mb.at[:, pl.ds(y_ * 2, 2), rows]

        return view

    def mix(q):
        def cols(n, _):
            at = pl.ds(pl.multiple_of(n * 256, 256), 256)
            out = jnp.dot(g[q].reshape(16 * S, DK), vw_out[:, at], preferred_element_type=F32)
            p1[q, :, :, :, at] = out.astype(BF16).reshape(4, 4, S, 256)
            return 0

        lax.fori_loop(0, DK // 256, cols, 0)

    def map_target(q, yg):
        out = jnp.dot(ta[q, yg].reshape(4 * S, DK), vproj[...], preferred_element_type=F32)
        p2[q, yg] = out.astype(BF16).reshape(2, 2, S, DC)

    def s_far(q):
        gather_dp_far(A0 + A_SLOTS * q, A[q], g_place(q), g_place2(q))

    def s_sib(q):
        gather_dp_sib(A0 + A_SLOTS * q, A[q], g_place(q), g_place2(q))

    def s_own(q):
        base = A0 + A_SLOTS * q
        A[q] = gather_dp_own(base, attn.at[pl.ds(q * S, S)], g_place(q), g_place2(q))

    def s_mix(q):
        own_a[q].wait()
        gather_dp_end(A[q])
        mix(q)
        B[q] = scatter_y_first(B0 + B_SLOTS * q, p1.at[q], y1.at[q])
        scatter_y_raw(B0 + B_SLOTS * q, B[q], p1.at[q], y2.at[q])

    def s_forward(q):
        scatter_y_forward(B0 + B_SLOTS * q, B[q], p1.at[q], y1.at[q], y2.at[q])

    def s_z(q):
        scatter_z(B0 + B_SLOTS * q, B[q], p1.at[q], y2.at[q], r.at[q], zr.at[q])

    def s_state(q):
        total = scatter_end(B[q], r.at[q], zr.at[q])
        state = total + vresid[pl.ds(q * S, S)].astype(F32)
        ta[q, y, zl] = state.astype(BF16)
        C[q] = gather_z(C0 + C_SLOTS * q, ta_view(q), early=True)

    def s_all_y(q):
        gather_y(C0 + C_SLOTS * q, C[q], ta_view(q))

    def s_all_forward(q):
        gather_forward(C0 + C_SLOTS * q, C[q], ta_view(q))

    def s_map(q):
        map_target(q, y)
        map_target(q, ring(y, 1))
        map_target(q, ring(y, 3))

    def s_target(q):
        gather_end(C[q])
        map_target(q, ring(y, 2))
        D[q]["s"] = send(D0 + D_SLOTS * q, p2.at[q, :, :, 1 - c], ds1.at[q], sib)

    def s_target_x(q):
        D[q]["s"].wait_recv()
        for i in range(4):
            for j in range(2):
                p3[q, i, j] = (p2[q, i, j, c].astype(F32) + ds1[q, i, j].astype(F32)).astype(BF16)
        for k in (1, 2, 3):
            D[q]["x", k] = send(D0 + D_SLOTS * q + k, p3.at[q, ring(x, k)], dx.at[q, k - 1], xs[k - 1])

    def s_target_z(q):
        for k in (1, 2, 3):
            D[q]["x", k].wait_recv()
        total = p3[q, x].astype(F32)
        for k in range(3):
            total += dx[q, k].astype(F32)
        p4[q] = total
        p4b[q] = total.astype(BF16)
        D[q]["z"] = send(D0 + D_SLOTS * q + 4, p4b.at[q, 1 - zh], dz.at[q], far)

    def s_mismatch(q):
        D[q]["z"].wait_recv()
        rows = pl.ds(q * S, S)
        target = p4[q, zh] + dz[q].astype(F32)
        diff = (vstud[rows].astype(F32) + so[rows] - target).astype(BF16)
        mt[q] = diff
        col = pl.multiple_of(t * DC, DC)
        ma[rows, pl.ds(col, DC)] = diff
        base = E0 + E_SLOTS * q
        cp = pltpu.make_async_remote_copy(
            mt.at[q], mb_view(q)(y, zl, 1), ss.at[base + 2 * E_GATHER], rs.at[base + 2 * E_GATHER],
            device_id=mirror, device_id_type=MESH,
        )

        @pl.when(d != t)
        def _():
            pltpu.make_async_remote_copy(
                mt.at[q], mb.at[lax.rem(d, 2), d // 2, rows], ss.at[base + 2 * E_GATHER], rs.at[base + 2 * E_GATHER],
                device_id=mirror, device_id_type=MESH,
            ).start()

        @pl.when(d == t)
        def _():
            mb[lax.rem(d, 2), d // 2, rows] = diff

        EM[q] = cp
        E[q] = gather_z(base, ma_view(q))

    def s_mirror(q):
        @pl.when(d != t)
        def _():
            EM[q].wait()

        base = E0 + E_SLOTS * q + E_GATHER
        EM[q] = gather_z(base, mb_view(q))

    def s_ey(q):
        gather_y(E0 + E_SLOTS * q, E[q], ma_view(q))

    def s_fy(q):
        gather_y(E0 + E_SLOTS * q + E_GATHER, EM[q], mb_view(q))

    def s_ef(q):
        gather_forward(E0 + E_SLOTS * q, E[q], ma_view(q))

    def s_ff(q):
        gather_forward(E0 + E_SLOTS * q + E_GATHER, EM[q], mb_view(q))

    def s_ee(q):
        gather_end(E[q])

    def s_fe(q):
        gather_end(EM[q])

    st = {}

    def ht_place(x_, zh_, c_):
        return ht.at[c_, :, pl.ds(pl.multiple_of((x_ * 2 + zh_) * TOK, TOK), TOK)]

    def ht_place2(x_, c_):
        return ht.at[c_, :, pl.ds(pl.multiple_of(x_ * 2 * TOK, 2 * TOK), 2 * TOK)]

    def student():
        l_gate.wait()
        l_up.wait()
        gf = vgate[...].astype(F32)
        h = (gf * jax.nn.sigmoid(gf) * vup[...].astype(F32)).astype(BF16)
        hid[...] = h
        l_down.wait()

        def cols(i, _):
            at = pl.ds(pl.multiple_of(i * DC, DC), DC)
            out = jnp.dot(hid[...], vw_down[:, at], preferred_element_type=F32)
            sp[i // 4, lax.rem(i, 4)] = out.astype(BF16)
            return 0

        lax.fori_loop(0, DS // DC, cols, 0)
        st["m"] = scatter_y_first(SB0, sp, sy1)
        scatter_y_raw(SB0, st["m"], sp, sy2)
        ht[c, :, pl.ds(pl.multiple_of((x * 2 + zh) * TOK, TOK), TOK)] = h.astype(F32).T.astype(BF16)

    def student_forward():
        scatter_y_forward(SB0, st["m"], sp, sy1, sy2)

    def student_z():
        scatter_z(SB0, st["m"], sp, sy2, sr, szr)

    def student_end():
        so[...] = scatter_end(st["m"], sr, szr)

    def hidden_own():
        st["h"] = gather_dp_own(H0, ht_place(x, zh, c), ht_place, ht_place2)

    def hidden_far():
        gather_dp_far(H0, st["h"], ht_place, ht_place2)

    def hidden_end():
        gather_dp_end(st["h"])

    def hidden_sib():
        gather_dp_sib(H0, st["h"], ht_place, ht_place2)

    def turn():
        def block(i, _):
            at = pl.ds(pl.multiple_of(i * 128, 128), 128)
            vturned[at, :] = vw_down[:, at].T
            return 0

        lax.fori_loop(0, DS // 128, block, 0)

    def gate_up():
        def cols(i, _):
            at = pl.ds(pl.multiple_of(i * 128, 128), 128)
            hg = jnp.dot(ma[...], vturned[:, at], preferred_element_type=F32)
            gf = vgate[:, at].astype(F32)
            uf = vup[:, at].astype(F32)
            sg = jax.nn.sigmoid(gf)
            gate_grad[:, at] = hg * uf * sg * (1.0 + gf * (1.0 - sg))
            up_grad[:, at] = hg * gf * sg
            return 0

        lax.fori_loop(0, FF // 128, cols, 0)

    def down():
        def block(i, _):
            at = pl.ds(pl.multiple_of(i * 448, 64), 448)
            out = jnp.dot(ht[0, at], mb[0].reshape(8 * TOK, DC), preferred_element_type=F32)
            out += jnp.dot(ht[1, at], mb[1].reshape(8 * TOK, DC), preferred_element_type=F32)
            down_grad[at] = out
            return 0

        lax.fori_loop(0, FF // 448, block, 0)

    waited = set()

    def once(cp):
        if id(cp) not in waited:
            waited.add(id(cp))
            cp.wait()

    steps = {
        "own": s_own, "far": s_far, "sib": s_sib, "mix": s_mix, "fwd": s_forward,
        "z": s_z, "state": s_state, "ally": s_all_y, "allf": s_all_forward, "map": s_map,
        "tgt": s_target, "tx": s_target_x, "tz": s_target_z, "mis": s_mismatch, "mir": s_mirror,
        "ey": s_ey, "fy": s_fy, "ef": s_ef, "ff": s_ff, "ee": s_ee, "fe": s_fe,
        "student": student, "stf": student_forward, "stz": student_z, "ste": student_end,
        "hown": hidden_own, "hfar": hidden_far, "hsib": hidden_sib, "hend": hidden_end,
        "turn": turn, "grads": gate_up, "down": down,
    }
    before = {"mix": l_out, "state": l_resid, "map": l_proj, "mis": l_stud}
    for step in ORDER:
        name, _, q = step.partition(".")
        if name in before:
            once(before[name])
        if q:
            steps[name](int(q))
        else:
            steps[name]()
    for cp in started:
        cp.wait_send()


def hand_out(a, b, c, a_out, b_out, c_out):
    a_out[...] = a[...]
    b_out[...] = b[...]
    c_out[...] = c[...]


def per_device(attn_out, teacher_resid, w_out, projection, student_in, gate_act, up_act, w_down):
    def vmem(*shape, dtype=BF16):
        return pltpu.VMEM(shape, dtype)

    grads = pl.pallas_call(
        kernel,
        out_shape=(
            jax.ShapeDtypeStruct((TOK, FF), F32),
            jax.ShapeDtypeStruct((TOK, FF), F32),
            jax.ShapeDtypeStruct((FF, DC), F32),
        ),
        in_specs=[pl.BlockSpec(memory_space=pl.ANY)] * 8,
        out_specs=(pl.BlockSpec(memory_space=pltpu.VMEM),) * 3,
        scratch_shapes=[
            vmem(Q, 4, 2, 2, S, DK),
            vmem(Q, 4, 4, S, DK),
            vmem(Q, 2, 2, S, DK),
            vmem(Q, 2, 4, S, DK),
            vmem(Q, 4, S, DK),
            vmem(Q, 3, S, DK),
            vmem(Q, 4, 4, S, DK),
            vmem(Q, 4, 2, 2, S, DC),
            vmem(Q, 4, 2, S, DC),
            vmem(Q, 4, 2, S, DC),
            vmem(Q, 3, 2, S, DC),
            vmem(Q, 2, S, DC, dtype=F32),
            vmem(Q, 2, S, DC),
            vmem(Q, S, DC),
            vmem(TOK, DS),
            vmem(Q, S, DC),
            vmem(2, 8, TOK, DC),
            vmem(TOK, FF),
            vmem(2, FF, 8 * TOK),
            vmem(4, 4, TOK, DC),
            vmem(2, 2, TOK, DC),
            vmem(2, 4, TOK, DC),
            vmem(4, TOK, DC),
            vmem(3, TOK, DC),
            vmem(TOK, DC, dtype=F32),
            vmem(DK, DK),
            vmem(DK, DC),
            vmem(FF, DS),
            vmem(DS, FF),
            vmem(TOK, DK),
            vmem(TOK, DC),
            vmem(TOK, FF),
            vmem(TOK, FF),
            pltpu.SemaphoreType.DMA((N_SLOTS,)),
            pltpu.SemaphoreType.DMA((N_SLOTS,)),
            pltpu.SemaphoreType.DMA((Q + 7,)),
        ],
        compiler_params=pltpu.CompilerParams(
            collective_id=0, has_side_effects=True, vmem_limit_bytes=58 * 2**20
        ),
        name="distill_step",
    )(attn_out, teacher_resid, w_out, projection, student_in, gate_act, up_act, w_down)
    return pl.pallas_call(
        hand_out,
        out_shape=tuple(jax.ShapeDtypeStruct(g.shape, g.dtype) for g in grads),
        in_specs=[pl.BlockSpec(memory_space=pltpu.VMEM)] * 3,
        out_specs=(pl.BlockSpec(memory_space=pltpu.VMEM),) * 3,
        name="hand_out",
    )(*grads)


def solution(mesh):
    in_specs = (
        P("dp", "tensor"),
        P("tensor", "dp"),
        P("tensor", "dp"),
        P("dp", "tensor"),
        P("dp", "tensor"),
        P("dp", "tensor"),
        P("dp", "tensor"),
        P("tensor", None),
    )
    out_specs = (P("dp", "tensor"), P("dp", "tensor"), P("tensor", "dp"))
    return jax.shard_map(
        per_device, mesh=mesh, in_specs=in_specs, out_specs=out_specs, check_vma=False
    )
```

profile of v0, /device:TPU:2, one launch (start us, length us, event | category | flops | bytes accessed | tf_op | source)
XLA Modules:
  0.0 151.9 jit_solution(17787341436605294677)
XLA Ops:
  0.6 148.5 %distill_step.1 = (f32[128,896]{1,0:T(8,128)}, f32[128,896]{1,0:T(8,128)}, f32[896,256]{1,0:T(8,128)}) custom-call(bf16[128,1024]{1,0:T(8,128)(2,1)} %attn.1, bf16[128,1024]{1,0:T(8,128)(2,1)} %resid.1, bf16[1024,1024]{1,0:T(8,128)(2,1)} %w_out.1, bf16[1024,256]{1,0:T(8,128)(2,1)} %proj.1, bf16[128,256]{1,0:T(8,128)(2,1)} %stud.1, bf16[128,896]{1,0:T(8,128)(2,1)} %gate.1, ...), custom_call_target="tpu_custom_call" | custom-call | tf_op jit(solution)/shard_map/distill_step/pallas_call | solution.py:480
  149.2 2.7 %hand_out.1 = (f32[128,896]{1,0:T(8,128)}, f32[128,896]{1,0:T(8,128)}, f32[896,256]{1,0:T(8,128)}) custom-call(f32[128,896]{1,0:T(8,128)} %get-tuple-element.6.a, f32[128,896]{1,0:T(8,128)} %get-tuple-element.7.b, f32[896,256]{1,0:T(8,128)} %get-tuple-element.8.c), custom_call_target="tpu_custom_call" | custom-call | tf_op jit(solution)/shard_map/hand_out/pallas_call | solution.py:532
where the time goes:
time: 152 us
  Pallas kernels  151 us (99%)
    pallas_call x1, Pallas kernels, per_device(): pl.pallas_call(kernel, out_shape=(jax.ShapeDtypeStruct((TOK, FF), F32), j...  149 us

commit v1 on v0

--- a/solution.py
+++ b/solution.py
@@ -18,10 +18,11 @@
 DC = 256
 DS = 4096
 FF = 896
-ORDER = ("own.0", "own.1", "student", "far.0", "own.2", "turn", "sib.0", "far.1", "own.3", "hown", "stf", "far.2", "mix.0", "sib.1", "stz", "far.3", "mix.1", "fwd.0", "fwd.1", "hfar", "z.0", "sib.2", "ste", "z.1", "mix.2", "sib.3", "state.0", "mix.3", "fwd.2", "state.1", "hsib", "fwd.3", "hend", "ally.0", "z.2", "ally.1", "z.3", "state.2", "allf.0", "map.0", "allf.1", "map.1", "state.3", "tgt.0", "tx.0", "ally.2", "tgt.1", "tx.1", "tz.0", "ally.3", "allf.2", "tz.1", "map.2", "mis.0", "mis.1", "mir.0", "ey.0", "allf.3", "map.3", "mir.1", "ey.1", "fy.0", "tgt.2", "fy.1", "ef.0", "tx.2", "tgt.3", "ef.1", "tz.2", "tx.3", "ff.0", "mis.2", "ff.1", "ee.0", "ee.1", "tz.3", "fe.0", "fe.1", "ey.2", "mir.2", "mis.3", "fy.2", "ef.2", "mir.3", "ey.3", "ff.2", "fy.3", "ee.2", "ef.3", "fe.2", "ff.3", "ee.3", "grads", "fe.3", "down")
-
-A_SLOTS, B_SLOTS, C_SLOTS, D_SLOTS, E_SLOTS = 12, 9, 13, 5, 15
-E_GATHER = 7
+ORDER = ("own.0", "hide", "sta", "far.0", "own.1", "own.2", "student", "sib.0", "far.1", "own.3", "mix.0", "sib.1", "far.2", "far.3", "hown", "fwd.0", "mix.1", "z.0", "sib.3", "fwd.1", "mix.3", "z.1", "hfar", "sib.2", "state.0", "fwd.3", "mix.2", "state.1", "fwd.2", "z.3", "stf", "ally.0", "z.2", "ally.1", "turn", "state.3", "allf.0", "allf.1", "state.2", "map.1", "hsib", "map.0", "tgt.0", "ally.3", "tgt.1", "stz", "ally.2", "tz.0", "allf.3", "tz.1", "ste", "allf.2", "mis.1", "map.2", "map.3", "tgt.3", "mis.0", "tgt.2", "hend", "ey.1", "fy.1", "ey.0", "tz.3", "fy.0", "ef.1", "tz.2", "ff.1", "mis.3", "ef.0", "ff.0", "fe.1", "mis.2", "ey.3", "fy.3", "ey.2", "fe.0", "fy.2", "ee.1", "ff.3", "ef.3", "ef.2", "ff.2", "ee.3", "fe.3", "ee.0", "ee.2", "grads", "fe.2", "down")
+
+A_SLOTS, B_SLOTS, C_SLOTS, D_SLOTS, E_SLOTS = 12, 9, 13, 8, 15
+E_GATHER = 4
+E_MIRROR = 11
 A0 = 0
 B0 = A0 + A_SLOTS * Q
 C0 = B0 + B_SLOTS * Q
@@ -35,7 +36,7 @@
 def kernel(
     attn, resid, w_out, proj, stud, gate, up, w_down,
     gate_grad, up_grad, down_grad,
-    g, p1, y1, y2, r, zr, ta, p2, ds1, p3, dx, p4, p4b, dz,
+    g, p1, y1, y2, r, zr, ta, p2, dx, p4, p4b, dz,
     ma, mt, mb, hid, ht, sp, sy1, sy2, sr, szr, so,
     vw_out, vproj, vw_down, vturned, vresid, vstud, vgate, vup,
     ss, rs, ls,
@@ -56,7 +57,10 @@
     xs = [dev(ring(x, k), zh, c, y, zl) for k in (1, 2, 3)]
     zs = [dev(x, zh, c, y, ring(zl, k)) for k in (1, 2, 3)]
     yn, yp = dev(x, zh, c, ring(y, 1), zl), dev(x, zh, c, ring(y, 3), zl)
-    mirror = (t, d)
+    xo = [dev(ring(x, k), zh, 1 - c, y, zl) for k in (1, 2, 3)]
+    mirror_to = [(t, (d // 4) * 4 + k) for k in range(4)]
+    mirror_from = [((t // 4) * 4 + k, d) for k in range(4)]
+    other = [jnp.logical_or(d != t, lax.rem(d, 4) != k) for k in range(4)]
 
     def load(i, src, dst):
         return pltpu.make_async_copy(src, dst, ls.at[i])
@@ -73,14 +77,15 @@
         cp.start()
 
     barrier = pltpu.get_barrier_semaphore()
-    for peer in [sib, far, yn, yp] + xs + zs:
+    for peer in [sib, far, yn, yp] + xs + xo + zs:
         pl.semaphore_signal(barrier, 1, device_id=peer, device_id_type=MESH)
-
-    @pl.when(d != t)
-    def _():
-        pl.semaphore_signal(barrier, 1, device_id=mirror, device_id_type=MESH)
-
-    pl.semaphore_wait(barrier, jnp.where(d != t, 11, 10))
+    for k in range(4):
+
+        @pl.when(other[k])
+        def _():
+            pl.semaphore_signal(barrier, 1, device_id=mirror_from[k], device_id_type=MESH)
+
+    pl.semaphore_wait(barrier, jnp.where(d != t, 17, 16))
 
     started = []
 
@@ -177,7 +182,8 @@
                 m["y1", k] = send(base + 4 + 2 * k, piece, piece, yp)
         else:
             for k in (1, 2, 3):
-                m["z", k].wait_recv()
+                if ("z", k) in m:
+                    m["z", k].wait_recv()
             mine = view(y, 0, 4)
             m["y0", 0] = send(base + 3, mine, mine, yn)
             m["y1", 0] = send(base + 4, mine, mine, yp)
@@ -285,25 +291,21 @@
     def s_target(q):
         gather_end(C[q])
         map_target(q, ring(y, 2))
-        D[q]["s"] = send(D0 + D_SLOTS * q, p2.at[q, :, :, 1 - c], ds1.at[q], sib)
-
-    def s_target_x(q):
-        D[q]["s"].wait_recv()
-        for i in range(4):
-            for j in range(2):
-                p3[q, i, j] = (p2[q, i, j, c].astype(F32) + ds1[q, i, j].astype(F32)).astype(BF16)
-        for k in (1, 2, 3):
-            D[q]["x", k] = send(D0 + D_SLOTS * q + k, p3.at[q, ring(x, k)], dx.at[q, k - 1], xs[k - 1])
+        base = D0 + D_SLOTS * q
+        for k in (1, 3, 2):
+            D[q][k - 1] = send(base + k - 1, p2.at[q, ring(x, k), :, c], dx.at[q, k - 1], xs[k - 1])
+            D[q][k + 2] = send(base + k + 2, p2.at[q, ring(x, k), :, 1 - c], dx.at[q, k + 2], xo[k - 1])
+        D[q][6] = send(base + 6, p2.at[q, x, :, 1 - c], dx.at[q, 6], sib)
 
     def s_target_z(q):
-        for k in (1, 2, 3):
-            D[q]["x", k].wait_recv()
-        total = p3[q, x].astype(F32)
-        for k in range(3):
+        for k in range(7):
+            D[q][k].wait_recv()
+        total = p2[q, x, :, c].astype(F32)
+        for k in range(7):
             total += dx[q, k].astype(F32)
         p4[q] = total
         p4b[q] = total.astype(BF16)
-        D[q]["z"] = send(D0 + D_SLOTS * q + 4, p4b.at[q, 1 - zh], dz.at[q], far)
+        D[q]["z"] = send(D0 + D_SLOTS * q + 7, p4b.at[q, 1 - zh], dz.at[q], far)
 
     def s_mismatch(q):
         D[q]["z"].wait_recv()
@@ -314,37 +316,37 @@
         col = pl.multiple_of(t * DC, DC)
         ma[rows, pl.ds(col, DC)] = diff
         base = E0 + E_SLOTS * q
-        cp = pltpu.make_async_remote_copy(
-            mt.at[q], mb_view(q)(y, zl, 1), ss.at[base + 2 * E_GATHER], rs.at[base + 2 * E_GATHER],
-            device_id=mirror, device_id_type=MESH,
-        )
-
-        @pl.when(d != t)
-        def _():
-            pltpu.make_async_remote_copy(
-                mt.at[q], mb.at[lax.rem(d, 2), d // 2, rows], ss.at[base + 2 * E_GATHER], rs.at[base + 2 * E_GATHER],
-                device_id=mirror, device_id_type=MESH,
-            ).start()
+        for k in range(4):
+
+            @pl.when(other[k])
+            def _():
+                mirror_copy(q, k, lax.rem(d, 4), d).start()
 
         @pl.when(d == t)
         def _():
             mb[lax.rem(d, 2), d // 2, rows] = diff
 
-        EM[q] = cp
         E[q] = gather_z(base, ma_view(q))
 
-    def s_mirror(q):
-        @pl.when(d != t)
-        def _():
-            EM[q].wait()
-
-        base = E0 + E_SLOTS * q + E_GATHER
-        EM[q] = gather_z(base, mb_view(q))
+    def mirror_copy(q, k, slot, owner):
+        base = E0 + E_SLOTS * q + E_MIRROR
+        return pltpu.make_async_remote_copy(
+            mt.at[q], mb.at[lax.rem(owner, 2), owner // 2, pl.ds(q * S, S)],
+            ss.at[base + k], rs.at[base + slot],
+            device_id=mirror_to[k], device_id_type=MESH,
+        )
 
     def s_ey(q):
         gather_y(E0 + E_SLOTS * q, E[q], ma_view(q))
 
     def s_fy(q):
+        for k in range(4):
+
+            @pl.when(other[k])
+            def _():
+                mirror_copy(q, k, k, (t // 4) * 4 + k).wait_recv()
+
+        EM[q] = {"early": False}
         gather_y(E0 + E_SLOTS * q + E_GATHER, EM[q], mb_view(q))
 
     def s_ef(q):
@@ -358,6 +360,11 @@
 
     def s_fe(q):
         gather_end(EM[q])
+        for k in range(4):
+
+            @pl.when(other[k])
+            def _():
+                mirror_copy(q, k, k, d).wait_send()
 
     st = {}
 
@@ -367,24 +374,31 @@
     def ht_place2(x_, c_):
         return ht.at[c_, :, pl.ds(pl.multiple_of(x_ * 2 * TOK, 2 * TOK), 2 * TOK)]
 
-    def student():
+    def hide():
         l_gate.wait()
         l_up.wait()
         gf = vgate[...].astype(F32)
         h = (gf * jax.nn.sigmoid(gf) * vup[...].astype(F32)).astype(BF16)
         hid[...] = h
-        l_down.wait()
-
+        ht[c, :, pl.ds(pl.multiple_of((x * 2 + zh) * TOK, TOK), TOK)] = h.astype(F32).T.astype(BF16)
+
+    def student_part(first, last):
         def cols(i, _):
             at = pl.ds(pl.multiple_of(i * DC, DC), DC)
             out = jnp.dot(hid[...], vw_down[:, at], preferred_element_type=F32)
             sp[i // 4, lax.rem(i, 4)] = out.astype(BF16)
             return 0
 
-        lax.fori_loop(0, DS // DC, cols, 0)
+        lax.fori_loop(first, last, cols, 0)
+
+    def student_a():
+        l_down.wait()
+        student_part(0, 8)
+
+    def student():
+        student_part(8, 16)
         st["m"] = scatter_y_first(SB0, sp, sy1)
         scatter_y_raw(SB0, st["m"], sp, sy2)
-        ht[c, :, pl.ds(pl.multiple_of((x * 2 + zh) * TOK, TOK), TOK)] = h.astype(F32).T.astype(BF16)
 
     def student_forward():
         scatter_y_forward(SB0, st["m"], sp, sy1, sy2)
@@ -448,9 +462,9 @@
     steps = {
         "own": s_own, "far": s_far, "sib": s_sib, "mix": s_mix, "fwd": s_forward,
         "z": s_z, "state": s_state, "ally": s_all_y, "allf": s_all_forward, "map": s_map,
-        "tgt": s_target, "tx": s_target_x, "tz": s_target_z, "mis": s_mismatch, "mir": s_mirror,
+        "tgt": s_target, "tz": s_target_z, "mis": s_mismatch,
         "ey": s_ey, "fy": s_fy, "ef": s_ef, "ff": s_ff, "ee": s_ee, "fe": s_fe,
-        "student": student, "stf": student_forward, "stz": student_z, "ste": student_end,
+        "hide": hide, "sta": student_a, "student": student, "stf": student_forward, "stz": student_z, "ste": student_end,
         "hown": hidden_own, "hfar": hidden_far, "hsib": hidden_sib, "hend": hidden_end,
         "turn": turn, "grads": gate_up, "down": down,
     }
@@ -495,9 +509,7 @@
             vmem(Q, 3, S, DK),
             vmem(Q, 4, 4, S, DK),
             vmem(Q, 4, 2, 2, S, DC),
-            vmem(Q, 4, 2, S, DC),
-            vmem(Q, 4, 2, S, DC),
-            vmem(Q, 3, 2, S, DC),
+            vmem(Q, 7, 2, S, DC),
             vmem(Q, 2, S, DC, dtype=F32),
             vmem(Q, 2, S, DC),
             vmem(Q, S, DC),

time: 152 us -> 142 us (0.934)
  Pallas kernels: 151 us -> 142 us
    pallas_call x1, Pallas kernels: 149 us -> 139 us  [per_device(): pl.pallas_call(kernel, out_shape=(jax.ShapeDtypeStruct((TOK, FF), F32), j...]
where the time goes in v1:
time: 142 us
  Pallas kernels  142 us (100%)
    pallas_call x1, Pallas kernels, per_device(): pl.pallas_call(kernel, out_shape=(jax.ShapeDtypeStruct((TOK, FF), F32), j...  139 us

profile of v1, /device:TPU:2, one launch (start us, length us, event | category | flops | bytes accessed | tf_op | source)
XLA Modules:
  0.0 142.3 jit_solution(15453425185034955606)
XLA Ops:
  0.6 138.9 %distill_step.1 = (f32[128,896]{1,0:T(8,128)}, f32[128,896]{1,0:T(8,128)}, f32[896,256]{1,0:T(8,128)}) custom-call(bf16[128,1024]{1,0:T(8,128)(2,1)} %attn.1, bf16[128,1024]{1,0:T(8,128)(2,1)} %resid.1, bf16[1024,1024]{1,0:T(8,128)(2,1)} %w_out.1, bf16[1024,256]{1,0:T(8,128)(2,1)} %proj.1, bf16[128,256]{1,0:T(8,128)(2,1)} %stud.1, bf16[128,896]{1,0:T(8,128)(2,1)} %gate.1, ...), custom_call_target="tpu_custom_call" | custom-call | tf_op jit(solution)/shard_map/distill_step/pallas_call | solution.py:494
  139.6 2.7 %hand_out.1 = (f32[128,896]{1,0:T(8,128)}, f32[128,896]{1,0:T(8,128)}, f32[896,256]{1,0:T(8,128)}) custom-call(f32[128,896]{1,0:T(8,128)} %get-tuple-element.6.a, f32[128,896]{1,0:T(8,128)} %get-tuple-element.7.b, f32[896,256]{1,0:T(8,128)} %get-tuple-element.8.c), custom_call_target="tpu_custom_call" | custom-call | tf_op jit(solution)/shard_map/hand_out/pallas_call | solution.py:544

commit v2 on v1

--- a/solution.py
+++ b/solution.py
@@ -23,6 +23,7 @@
 A_SLOTS, B_SLOTS, C_SLOTS, D_SLOTS, E_SLOTS = 12, 9, 13, 8, 15
 E_GATHER = 4
 E_MIRROR = 11
+IN_FLIGHT = 60
 A0 = 0
 B0 = A0 + A_SLOTS * Q
 C0 = B0 + B_SLOTS * Q
@@ -35,8 +36,8 @@
 
 def kernel(
     attn, resid, w_out, proj, stud, gate, up, w_down,
-    gate_grad, up_grad, down_grad,
-    g, p1, y1, y2, r, zr, ta, p2, dx, p4, p4b, dz,
+    gate_out, up_out, down_out,
+    gate_grad, up_grad, down_grad, g, p1, y1, y2, r, zr, ta, p2, dx, p4, p4b, dz,
     ma, mt, mb, hid, ht, sp, sy1, sy2, sr, szr, so,
     vw_out, vproj, vw_down, vturned, vresid, vstud, vgate, vup,
     ss, rs, ls,
@@ -75,6 +76,10 @@
     l_stud = load(Q + 6, stud, vstud)
     for cp in [l_gate, l_up, l_down, l_out] + own_a + [l_proj, l_resid, l_stud]:
         cp.start()
+
+    out_copies = [
+        load(Q + 7, gate_grad, gate_out), load(Q + 8, up_grad, up_out), load(Q + 9, down_grad, down_out),
+    ]
 
     barrier = pltpu.get_barrier_semaphore()
     for peer in [sib, far, yn, yp] + xs + xo + zs:
@@ -354,17 +359,17 @@
 
     def s_ff(q):
         gather_forward(E0 + E_SLOTS * q + E_GATHER, EM[q], mb_view(q))
-
-    def s_ee(q):
-        gather_end(E[q])
-
-    def s_fe(q):
-        gather_end(EM[q])
         for k in range(4):
 
             @pl.when(other[k])
             def _():
                 mirror_copy(q, k, k, d).wait_send()
+
+    def s_ee(q):
+        gather_end(E[q])
+
+    def s_fe(q):
+        gather_end(EM[q])
 
     st = {}
 
@@ -441,6 +446,8 @@
             return 0
 
         lax.fori_loop(0, FF // 128, cols, 0)
+        for cp in out_copies[:2]:
+            cp.start()
 
     def down():
         def block(i, _):
@@ -451,6 +458,7 @@
             return 0
 
         lax.fori_loop(0, FF // 448, block, 0)
+        out_copies[2].start()
 
     waited = set()
 
@@ -477,14 +485,28 @@
             steps[name](int(q))
         else:
             steps[name]()
+        while len(started) > IN_FLIGHT:
+            started.pop(0).wait_send()
     for cp in started:
         cp.wait_send()
-
-
-def hand_out(a, b, c, a_out, b_out, c_out):
-    a_out[...] = a[...]
-    b_out[...] = b[...]
-    c_out[...] = c[...]
+    for cp in out_copies:
+        cp.wait()
+
+
+def hand_out(a, b, c, a_out, b_out, c_out, a_held, b_held, c_held, sem):
+    held = (a_held, b_held, c_held)
+    ins = [pltpu.make_async_copy(src, v, sem.at[i]) for i, (src, v) in enumerate(zip((a, b, c), held))]
+    outs = [
+        pltpu.make_async_copy(v, dst, sem.at[3 + i])
+        for i, (v, dst) in enumerate(zip(held, (a_out, b_out, c_out)))
+    ]
+    for cp in ins:
+        cp.start()
+    for first, then in zip(ins, outs):
+        first.wait()
+        then.start()
+    for cp in outs:
+        cp.wait()
 
 
 def per_device(attn_out, teacher_resid, w_out, projection, student_in, gate_act, up_act, w_down):
@@ -499,8 +521,11 @@
             jax.ShapeDtypeStruct((FF, DC), F32),
         ),
         in_specs=[pl.BlockSpec(memory_space=pl.ANY)] * 8,
-        out_specs=(pl.BlockSpec(memory_space=pltpu.VMEM),) * 3,
+        out_specs=(pl.BlockSpec(memory_space=pl.ANY),) * 3,
         scratch_shapes=[
+            vmem(TOK, FF, dtype=F32),
+            vmem(TOK, FF, dtype=F32),
+            vmem(FF, DC, dtype=F32),
             vmem(Q, 4, 2, 2, S, DK),
             vmem(Q, 4, 4, S, DK),
             vmem(Q, 2, 2, S, DK),
@@ -534,7 +559,7 @@
             vmem(TOK, FF),
             pltpu.SemaphoreType.DMA((N_SLOTS,)),
             pltpu.SemaphoreType.DMA((N_SLOTS,)),
-            pltpu.SemaphoreType.DMA((Q + 7,)),
+            pltpu.SemaphoreType.DMA((Q + 10,)),
         ],
         compiler_params=pltpu.CompilerParams(
             collective_id=0, has_side_effects=True, vmem_limit_bytes=58 * 2**20
@@ -544,8 +569,9 @@
     return pl.pallas_call(
         hand_out,
         out_shape=tuple(jax.ShapeDtypeStruct(g.shape, g.dtype) for g in grads),
-        in_specs=[pl.BlockSpec(memory_space=pltpu.VMEM)] * 3,
-        out_specs=(pl.BlockSpec(memory_space=pltpu.VMEM),) * 3,
+        in_specs=[pl.BlockSpec(memory_space=pl.ANY)] * 3,
+        out_specs=(pl.BlockSpec(memory_space=pl.ANY),) * 3,
+        scratch_shapes=[pltpu.VMEM(g.shape, g.dtype) for g in grads] + [pltpu.SemaphoreType.DMA((6,))],
         name="hand_out",
     )(*grads)
 

time: 142 us -> 141 us (level)
  no operation moved by 1% of the time
where the time goes in v2:
time: 141 us
  Pallas kernels  141 us (100%)
    pallas_call x1, Pallas kernels, per_device(): pl.pallas_call(kernel, out_shape=(jax.ShapeDtypeStruct((TOK, FF), F32), j...  138 us

profile of v2, /device:TPU:2, one launch (start us, length us, event | category | flops | bytes accessed | tf_op | source)
XLA Modules:
  0.0 141.3 jit_solution(9634874648876871272)
XLA Ops:
  0.6 138.3 %distill_step.1 = (f32[128,896]{1,0:T(8,128)}, f32[128,896]{1,0:T(8,128)}, f32[896,256]{1,0:T(8,128)}) custom-call(bf16[128,1024]{1,0:T(8,128)(2,1)} %attn.1, bf16[128,1024]{1,0:T(8,128)(2,1)} %resid.1, bf16[1024,1024]{1,0:T(8,128)(2,1)} %w_out.1, bf16[1024,256]{1,0:T(8,128)(2,1)} %proj.1, bf16[128,256]{1,0:T(8,128)(2,1)} %stud.1, bf16[128,896]{1,0:T(8,128)(2,1)} %gate.1, ...), custom_call_target="tpu_custom_call" | custom-call | tf_op jit(solution)/shard_map/distill_step/pallas_call | solution.py:516
  138.9 2.4 %hand_out.1 = (f32[128,896]{1,0:T(8,128)}, f32[128,896]{1,0:T(8,128)}, f32[896,256]{1,0:T(8,128)}) custom-call(f32[128,896]{1,0:T(8,128)} %get-tuple-element.6.a, f32[128,896]{1,0:T(8,128)} %get-tuple-element.7.b, f32[896,256]{1,0:T(8,128)} %get-tuple-element.8.c), custom_call_target="tpu_custom_call" | custom-call | tf_op jit(solution)/shard_map/hand_out/pallas_call | solution.py:569

commit v3 on v2

--- a/solution.py
+++ b/solution.py
@@ -18,7 +18,7 @@
 DC = 256
 DS = 4096
 FF = 896
-ORDER = ("own.0", "hide", "sta", "far.0", "own.1", "own.2", "student", "sib.0", "far.1", "own.3", "mix.0", "sib.1", "far.2", "far.3", "hown", "fwd.0", "mix.1", "z.0", "sib.3", "fwd.1", "mix.3", "z.1", "hfar", "sib.2", "state.0", "fwd.3", "mix.2", "state.1", "fwd.2", "z.3", "stf", "ally.0", "z.2", "ally.1", "turn", "state.3", "allf.0", "allf.1", "state.2", "map.1", "hsib", "map.0", "tgt.0", "ally.3", "tgt.1", "stz", "ally.2", "tz.0", "allf.3", "tz.1", "ste", "allf.2", "mis.1", "map.2", "map.3", "tgt.3", "mis.0", "tgt.2", "hend", "ey.1", "fy.1", "ey.0", "tz.3", "fy.0", "ef.1", "tz.2", "ff.1", "mis.3", "ef.0", "ff.0", "fe.1", "mis.2", "ey.3", "fy.3", "ey.2", "fe.0", "fy.2", "ee.1", "ff.3", "ef.3", "ef.2", "ff.2", "ee.3", "fe.3", "ee.0", "ee.2", "grads", "fe.2", "down")
+ORDER = ("own.0", "hide", "sta", "far.0", "own.1", "own.2", "student", "sib.0", "far.1", "own.3", "mix.0", "sib.1", "far.2", "far.3", "hown", "fwd.0", "mix.1", "z.0", "sib.3", "fwd.1", "mix.3", "z.1", "hfar", "sib.2", "state.0", "fwd.3", "mix.2", "state.1", "fwd.2", "z.3", "stf", "ally.0", "z.2", "ally.1", "turn", "state.3", "allf.0", "allf.1", "state.2", "map.1", "hsib", "map.0", "tgt.0", "ally.3", "tgt.1", "stz", "ally.2", "tz.0", "allf.3", "tz.1", "ste", "allf.2", "mis.1", "map.2", "map.3", "tgt.3", "mis.0", "tgt.2", "hend", "ey.1", "fy.1", "ey.0", "tz.3", "fy.0", "ef.1", "tz.2", "ff.1", "mis.3", "ef.0", "ff.0", "fe.1", "mis.2", "ey.3", "fy.3", "ey.2", "fe.0", "fy.2", "ee.1", "ff.3", "ef.3", "ef.2", "ff.2", "grada", "downa", "ee.3", "fe.3", "ee.0", "ee.2", "grads", "fe.2", "down")
 
 A_SLOTS, B_SLOTS, C_SLOTS, D_SLOTS, E_SLOTS = 12, 9, 13, 8, 15
 E_GATHER = 4
@@ -434,10 +434,23 @@
 
         lax.fori_loop(0, DS // 128, block, 0)
 
+    def hidden_part(at, y_):
+        k = pl.ds(pl.multiple_of(y_ * 4 * DC, 4 * DC), 4 * DC)
+        return jnp.dot(ma[:, k], vturned[k, at], preferred_element_type=F32)
+
+    def gate_up_near():
+        def cols(i, _):
+            at = pl.ds(pl.multiple_of(i * 128, 128), 128)
+            near = hidden_part(at, y) + hidden_part(at, ring(y, 1)) + hidden_part(at, ring(y, 3))
+            gate_grad[:, at] = near
+            return 0
+
+        lax.fori_loop(0, FF // 128, cols, 0)
+
     def gate_up():
         def cols(i, _):
             at = pl.ds(pl.multiple_of(i * 128, 128), 128)
-            hg = jnp.dot(ma[...], vturned[:, at], preferred_element_type=F32)
+            hg = gate_grad[:, at] + hidden_part(at, ring(y, 2))
             gf = vgate[:, at].astype(F32)
             uf = vup[:, at].astype(F32)
             sg = jax.nn.sigmoid(gf)
@@ -449,12 +462,27 @@
         for cp in out_copies[:2]:
             cp.start()
 
+    def down_part(at, x_):
+        k = pl.ds(pl.multiple_of(x_ * 2 * TOK, 2 * TOK), 2 * TOK)
+        rows = pl.ds(x_ * 2, 2)
+        out = jnp.dot(ht[0, at, k], mb[0, rows].reshape(2 * TOK, DC), preferred_element_type=F32)
+        return out + jnp.dot(
+            ht[1, at, k], mb[1, rows].reshape(2 * TOK, DC), preferred_element_type=F32
+        )
+
+    def down_near():
+        def block(i, _):
+            at = pl.ds(pl.multiple_of(i * 448, 64), 448)
+            near = down_part(at, y) + down_part(at, ring(y, 1)) + down_part(at, ring(y, 3))
+            down_grad[at] = near
+            return 0
+
+        lax.fori_loop(0, FF // 448, block, 0)
+
     def down():
         def block(i, _):
             at = pl.ds(pl.multiple_of(i * 448, 64), 448)
-            out = jnp.dot(ht[0, at], mb[0].reshape(8 * TOK, DC), preferred_element_type=F32)
-            out += jnp.dot(ht[1, at], mb[1].reshape(8 * TOK, DC), preferred_element_type=F32)
-            down_grad[at] = out
+            down_grad[at] = down_grad[at] + down_part(at, ring(y, 2))
             return 0
 
         lax.fori_loop(0, FF // 448, block, 0)
@@ -474,7 +502,7 @@
         "ey": s_ey, "fy": s_fy, "ef": s_ef, "ff": s_ff, "ee": s_ee, "fe": s_fe,
         "hide": hide, "sta": student_a, "student": student, "stf": student_forward, "stz": student_z, "ste": student_end,
         "hown": hidden_own, "hfar": hidden_far, "hsib": hidden_sib, "hend": hidden_end,
-        "turn": turn, "grads": gate_up, "down": down,
+        "turn": turn, "grada": gate_up_near, "downa": down_near, "grads": gate_up, "down": down,
     }
     before = {"mix": l_out, "state": l_resid, "map": l_proj, "mis": l_stud}
     for step in ORDER:

time: 141 us -> 141 us (level); the launches traced: 141 us -> 139 us
  Pallas kernels: 141 us -> 138 us
    pallas_call x1, Pallas kernels: 138 us -> 136 us  [per_device(): pl.pallas_call(kernel, out_shape=(jax.ShapeDtypeStruct((TOK, FF), F32), j...]
where the time goes in v3:
time: 141 us; the launch traced here: 139 us
  Pallas kernels  138 us (98%)
    pallas_call x1, Pallas kernels, per_device(): pl.pallas_call(kernel, out_shape=(jax.ShapeDtypeStruct((TOK, FF), F32), j...  136 us

profile of v3, /device:TPU:2, one launch (start us, length us, event | category | flops | bytes accessed | tf_op | source)
XLA Modules:
  0.0 139.1 jit_solution(3750544044027722234)
XLA Ops:
  0.6 136.1 %distill_step.1 = (f32[128,896]{1,0:T(8,128)}, f32[128,896]{1,0:T(8,128)}, f32[896,256]{1,0:T(8,128)}) custom-call(bf16[128,1024]{1,0:T(8,128)(2,1)} %attn.1, bf16[128,1024]{1,0:T(8,128)(2,1)} %resid.1, bf16[1024,1024]{1,0:T(8,128)(2,1)} %w_out.1, bf16[1024,256]{1,0:T(8,128)(2,1)} %proj.1, bf16[128,256]{1,0:T(8,128)(2,1)} %stud.1, bf16[128,896]{1,0:T(8,128)(2,1)} %gate.1, ...), custom_call_target="tpu_custom_call" | custom-call | tf_op jit(solution)/shard_map/distill_step/pallas_call | solution.py:544
  136.7 2.4 %hand_out.1 = (f32[128,896]{1,0:T(8,128)}, f32[128,896]{1,0:T(8,128)}, f32[896,256]{1,0:T(8,128)}) custom-call(f32[128,896]{1,0:T(8,128)} %get-tuple-element.6.a, f32[128,896]{1,0:T(8,128)} %get-tuple-element.7.b, f32[896,256]{1,0:T(8,128)} %get-tuple-element.8.c), custom_call_target="tpu_custom_call" | custom-call | tf_op jit(solution)/shard_map/hand_out/pallas_call | solution.py:597

commit v4 on v3

--- a/solution.py
+++ b/solution.py
@@ -18,7 +18,7 @@
 DC = 256
 DS = 4096
 FF = 896
-ORDER = ("own.0", "hide", "sta", "far.0", "own.1", "own.2", "student", "sib.0", "far.1", "own.3", "mix.0", "sib.1", "far.2", "far.3", "hown", "fwd.0", "mix.1", "z.0", "sib.3", "fwd.1", "mix.3", "z.1", "hfar", "sib.2", "state.0", "fwd.3", "mix.2", "state.1", "fwd.2", "z.3", "stf", "ally.0", "z.2", "ally.1", "turn", "state.3", "allf.0", "allf.1", "state.2", "map.1", "hsib", "map.0", "tgt.0", "ally.3", "tgt.1", "stz", "ally.2", "tz.0", "allf.3", "tz.1", "ste", "allf.2", "mis.1", "map.2", "map.3", "tgt.3", "mis.0", "tgt.2", "hend", "ey.1", "fy.1", "ey.0", "tz.3", "fy.0", "ef.1", "tz.2", "ff.1", "mis.3", "ef.0", "ff.0", "fe.1", "mis.2", "ey.3", "fy.3", "ey.2", "fe.0", "fy.2", "ee.1", "ff.3", "ef.3", "ef.2", "ff.2", "grada", "downa", "ee.3", "fe.3", "ee.0", "ee.2", "grads", "fe.2", "down")
+ORDER = ("own.0", "hide", "sta", "far.0", "own.1", "student", "sib.0", "own.2", "far.1", "own.3", "mix.0", "sib.1", "far.2", "far.3", "hown", "fwd.0", "mix.1", "z.0", "sib.3", "fwd.1", "mix.3", "z.1", "hfar", "sib.2", "state.0", "fwd.3", "mix.2", "state.1", "fwd.2", "z.3", "stf", "ally.0", "z.2", "ally.1", "turn", "state.3", "allf.0", "allf.1", "state.2", "map.1", "hsib", "map.0", "tgt.0", "ally.3", "tgt.1", "stz", "ally.2", "tz.0", "allf.3", "tz.1", "ste", "allf.2", "mis.1", "map.2", "map.3", "tgt.3", "mis.0", "tgt.2", "hend", "ey.1", "fy.1", "ey.0", "tz.3", "fy.0", "ef.1", "tz.2", "ff.1", "mis.3", "ef.0", "ff.0", "fe.1", "mis.2", "ey.3", "fy.3", "ey.2", "fe.0", "fy.2", "ee.1", "ff.3", "ef.3", "ef.2", "ff.2", "grada", "downa", "ee.3", "fe.3", "ee.0", "ee.2", "grads", "fe.2", "down")
 
 A_SLOTS, B_SLOTS, C_SLOTS, D_SLOTS, E_SLOTS = 12, 9, 13, 8, 15
 E_GATHER = 4

time: 141 us -> 142 us (level)
  Pallas kernels: 138 us -> 140 us
    pallas_call x1, Pallas kernels: 136 us -> 138 us  [per_device(): pl.pallas_call(kernel, out_shape=(jax.ShapeDtypeStruct((TOK, FF), F32), j...]
where the time goes in v4:
time: 142 us; the launch traced here: 141 us
  Pallas kernels  140 us (99%)
    pallas_call x1, Pallas kernels, per_device(): pl.pallas_call(kernel, out_shape=(jax.ShapeDtypeStruct((TOK, FF), F32), j...  138 us

profile of v4, /device:TPU:2, one launch (start us, length us, event | category | flops | bytes accessed | tf_op | source)
XLA Modules:
  0.0 140.8 jit_solution(17609338567029114826)
XLA Ops:
  0.6 137.8 %distill_step.1 = (f32[128,896]{1,0:T(8,128)}, f32[128,896]{1,0:T(8,128)}, f32[896,256]{1,0:T(8,128)}) custom-call(bf16[128,1024]{1,0:T(8,128)(2,1)} %attn.1, bf16[128,1024]{1,0:T(8,128)(2,1)} %resid.1, bf16[1024,1024]{1,0:T(8,128)(2,1)} %w_out.1, bf16[1024,256]{1,0:T(8,128)(2,1)} %proj.1, bf16[128,256]{1,0:T(8,128)(2,1)} %stud.1, bf16[128,896]{1,0:T(8,128)(2,1)} %gate.1, ...), custom_call_target="tpu_custom_call" | custom-call | tf_op jit(solution)/shard_map/distill_step/pallas_call | solution.py:544
  138.4 2.4 %hand_out.1 = (f32[128,896]{1,0:T(8,128)}, f32[128,896]{1,0:T(8,128)}, f32[896,256]{1,0:T(8,128)}) custom-call(f32[128,896]{1,0:T(8,128)} %get-tuple-element.6.a, f32[128,896]{1,0:T(8,128)} %get-tuple-element.7.b, f32[896,256]{1,0:T(8,128)} %get-tuple-element.8.c), custom_call_target="tpu_custom_call" | custom-call | tf_op jit(solution)/shard_map/hand_out/pallas_call | solution.py:597
